TPU v7x, 128 devices: a whole 4x4x4 slice. The times are simulated.
128 devices in a mesh: scene: 8 (over y, core), frame: 16 (over z, x).
Axes of the slice: x: 4, y: 4, z: 4, core: 2. Of those that a mesh axis runs over, the one named last changes fastest.
Arguments:
- occupancy: bfloat16 [8, 64, 64, 2048], P('scene', 'frame'), may hold values from -6 to 6
- scene_lengths: int32 [8], P('scene'), may hold values from 8 to 64, as said below
- conv1_weight: bfloat16 [128, 1728], replicated, may hold values from -0.15625 to 0.15625
- conv2_weight: bfloat16 [256, 3456], replicated, may hold values from -0.109375 to 0.109375
- temporal_weight: bfloat16 [3, 256, 256], replicated, may hold values from -0.21875 to 0.21875
- query_weight: bfloat16 [256, 256], replicated
- key_weight: bfloat16 [256, 256], replicated
- value_weight: bfloat16 [256, 256], replicated, may hold values from -0.375 to 0.375
- out_weight: bfloat16 [256, 256], replicated, may hold values from -0.375 to 0.375
Outputs:
- encoded: bfloat16 [8, 64, 256, 512], P('scene', 'frame')
- kl_loss: float32 [], replicated
Inputs may be any that keep to these rules, and one draw needn't show every extreme that they name: `scene_lengths`: non-decreasing along the scenes; the first scene has exactly 8 frames with data and the last exactly 64.
All inputs are finite; a program needn't handle non-finite values.
Results may differ from a plain program's by a relative error of at most 0.011.
Values may be sent and summed in bfloat16 or wider, within the bound.
A program may use at most 192 MiB of HBM per device.

v0:
```python
import jax
import jax.numpy as jnp
from jax import lax
from jax.sharding import PartitionSpec as P

CIN = 64
C1 = 128
C2 = 256
HEADS = 4
HD = 64
HI = 16
ZD = 8
CELLS = 512
NORM_EPS = 1e-06


def extended(cells, sides, width):
    for axis, dim in sides:
        count = lax.axis_size(axis)
        ends = count - 1
        head = lax.slice_in_dim(cells, 0, width, axis=dim)
        tail = lax.slice_in_dim(cells, cells.shape[dim] - width, cells.shape[dim], axis=dim)
        cells = jnp.concatenate(
            [
                lax.ppermute(tail, axis, [(i, (i + 1) % count) for i in range(ends)]),
                cells,
                lax.ppermute(head, axis, [((i + 1) % count, i) for i in range(ends)]),
            ],
            axis=dim,
        )
    return cells


def spatial_conv(voxels, weight, channels_in, stride):
    channels_out = weight.shape[0]
    kernel = weight.reshape(channels_out, channels_in, 3, 3, 3)
    return lax.conv_general_dilated(
        voxels,
        kernel,
        (stride, stride, 1),
        ((1, 1), (1, 1), (1, 1)),
        dimension_numbers=("NCDHW", "OIDHW", "NCDHW"),
        preferred_element_type=jnp.float32,
    )


def mix_channels(weight, maps):
    return jnp.einsum("oc,fcn->fon", weight, maps, preferred_element_type=jnp.float32)


def temporal_block(padded, second_maps, temporal_weight):
    count_frames = second_maps.shape[0]
    temporal_sum = mix_channels(temporal_weight[0], padded[0:count_frames])
    for tap in range(1, 3):
        temporal_sum = temporal_sum + mix_channels(
            temporal_weight[tap], padded[tap : tap + count_frames]
        )
    residual_maps = (second_maps.astype(jnp.float32) + jax.nn.silu(temporal_sum)).astype(
        jnp.bfloat16
    )
    return residual_maps.astype(jnp.float32)


def project_rows(residual_f, query_weight, key_weight, value_weight):
    count_frames = residual_f.shape[0]
    count_cells = residual_f.shape[2]
    normed = (
        residual_f * lax.rsqrt(jnp.mean(residual_f * residual_f, axis=1, keepdims=True) + NORM_EPS)
    ).astype(jnp.bfloat16)
    queries = (
        mix_channels(query_weight, normed)
        .astype(jnp.bfloat16)
        .reshape(count_frames, HEADS, HD, count_cells)
    )
    key_rows = (
        mix_channels(key_weight, normed)
        .astype(jnp.bfloat16)
        .reshape(count_frames, HEADS, HD, count_cells)
    )
    value_rows = (
        mix_channels(value_weight, normed)
        .astype(jnp.bfloat16)
        .reshape(count_frames, HEADS, HD, count_cells)
    )
    return (queries, key_rows, value_rows)


def finish_rows(residual_f, attended, out_weight, valid_rows):
    count_frames = residual_f.shape[0]
    count_cells = residual_f.shape[2]
    out_full = residual_f + mix_channels(
        out_weight, attended.reshape(count_frames, C2, count_cells)
    )
    return (out_full * valid_rows[:, None, None]).astype(jnp.bfloat16)


def shards(
    occupancy,
    scene_lengths,
    conv1_weight,
    conv2_weight,
    temporal_weight,
    query_weight,
    key_weight,
    value_weight,
    out_weight,
):
    f_dev = occupancy.shape[1]
    length = scene_lengths[0]
    first_frame = lax.axis_index("frame") * f_dev
    frame_ids = first_frame + jnp.arange(f_dev, dtype=jnp.int32)
    valid_rows = (frame_ids < length).astype(jnp.float32)
    voxels = occupancy[0].reshape(f_dev, CIN, HI, HI, ZD)
    first_maps = jax.nn.silu(spatial_conv(voxels, conv1_weight, CIN, 2)).astype(jnp.bfloat16)
    second_full = jax.nn.silu(spatial_conv(first_maps, conv2_weight, C1, 1))
    second_maps = (second_full.reshape(f_dev, C2, CELLS) * valid_rows[:, None, None]).astype(
        jnp.bfloat16
    )
    padded = extended(second_maps, (("frame", 0),), 1)
    residual_f = temporal_block(padded, second_maps, temporal_weight)
    queries, key_rows, value_rows = project_rows(residual_f, query_weight, key_weight, value_weight)
    running_max = jnp.full((f_dev, HEADS, CELLS), -1e30, jnp.float32)
    panel_keys = lax.all_gather(key_rows, "frame", axis=0, tiled=True)
    panel_values = lax.all_gather(value_rows, "frame", axis=0, tiled=True)
    count_keys = panel_keys.shape[0]
    scores = jnp.einsum(
        "qhdc,khdc->qkhc", queries, panel_keys, preferred_element_type=jnp.float32
    ) * HD ** (-0.5)
    key_mask = (jnp.arange(count_keys) < length)[None, :, None, None]
    scores = jnp.where(key_mask, scores, -1e30)
    new_max = jnp.maximum(running_max, jnp.max(scores, axis=1))
    raw_weights = jnp.where(key_mask, jnp.exp(scores - new_max[:, None]), 0.0)
    new_sum = jnp.sum(raw_weights, axis=1)
    addition = jnp.einsum(
        "qkhc,khdc->qhdc",
        raw_weights.astype(jnp.bfloat16),
        panel_values,
        preferred_element_type=jnp.float32,
    )
    attended = (addition / new_sum[:, :, None, :]).astype(jnp.bfloat16)
    encoded = finish_rows(residual_f, attended, out_weight, valid_rows)
    squares = jnp.sum(jnp.square(encoded.astype(jnp.float32)))
    grand_total = lax.psum(squares, ("scene", "frame"))
    slot_count = float(lax.axis_size("scene") * lax.axis_size("frame") * f_dev * CELLS * C2)
    kl_loss = 0.5 * grand_total / slot_count
    return (encoded[None], kl_loss)


def solution(mesh):
    placed = (P("scene", "frame", None, None), P("scene"), P(), P(), P(), P(), P(), P(), P())
    return jax.shard_map(
        shards,
        mesh=mesh,
        in_specs=placed,
        out_specs=(P("scene", "frame", None, None), P()),
        check_vma=False,
    )
```

profile of v0, /device:TPU:1, one launch (start us, length us, event | category | flops | bytes accessed | tf_op | source)
XLA Modules:
  0.0 420.5 jit_solution(17460069256639030074)
XLA Ops:
  7.2 0.0 copy-start
  7.2 0.0 all-gather.5.cloned.1.call-start
  7.9 2.6 copy.62
  10.5 0.0 copy-start.3
  10.6 2.9 reshape.49
  13.4 0.0 copy-done.3
  13.4 1.1 copy.59
  14.5 1.5 reshape.48
  16.0 0.0 copy-start.1
  16.0 5.0 %fusion.28 = bf16[4,128,8,8,8]{1,0,4,3,2:T(4,128)(2,1)S(1)} fusion(bf16[4,64,16,16,8]{1,4,3,2,0:T(8,128)(2,1)S(1)} %bitcast.90, bf16[128,64,3,3,3]{0,4,3,2,1:T(4,128)(2,1)S(1)} %reshape.48), kind=kOutput, calls=%fused_computation.44 | convolution fusion | flops 764018688 | bytes 2015232 | tf_op jit(solution)/shard_map/conv_general_dilated | solution.py:37
  21.0 0.0 copy-done.1
  21.0 7.9 %multiply_convert_fusion = (bf16[4,256,8,8,8]{1,0,4,3,2:T(4,128)(2,1)S(1)}, f32[4,256,8,8,8]{1,0,4,3,2:T(4,128)}) fusion(f32[4]{0:T(128)S(1)} %compare_convert_fusion, bf16[4,128,8,8,8]{1,0,4,3,2:T(4,128)(2,1)S(1)} %fusion.28, bf16[256,128,3,3,3]{0,4,3,2,1:T(4,128)(2,1)S(1)} %copy-done.1), kind=kOutput, calls=%fused_computation.24 | convolution fusion | flops 2794455040 | bytes 5439504 | tf_op jit(solution)/shard_map/conv_general_dilated | solution.py:37
  28.9 1.9 copy.64
  30.8 0.0 copy-start.4
  30.8 0.3 multiply_convert_fusion.1
  31.2 4.0 collective-permute-start
  35.1 1.5 collective-permute-start.1
  36.6 0.0 copy-done.4
  36.6 0.5 fusion.26
  37.1 3.0 collective-permute-done
  40.1 0.4 fusion.24
  40.5 0.0 copy-start.5
  40.5 3.4 collective-permute-done.1
  43.9 1.1 fusion.2
  44.9 0.0 copy-start.6
  45.0 0.0 copy-done.5
  45.0 1.4 convolution_convert_fusion.1
  46.4 0.0 copy-start.7
  46.4 0.0 all-gather.5.cloned.1.call-update
  46.4 0.0 all-gather.3.cloned.1.call-start
  46.5 0.0 copy-done.6
  46.5 1.4 convolution_convert_fusion.2
  47.9 0.0 all-gather.3.cloned.1.call-update
  48.0 0.0 copy-done.7
  48.0 0.5 convolution_convert_fusion
  48.4 2.5 copy.67
  50.9 0.0 copy-start.2
  50.9 112.4 %all-gather.5.cloned.1.call-done = bf16[64,4,64,512]{3,2,1,0:T(8,128)(2,1)} async-done(((bf16[4,4,64,512]{3,2,1,0:T(8,128)(2,1)}), bf16[64,4,64,512]{3,2,1,0:T(8,128)(2,1)}) %all-gather.5.cloned.1.call-update) | async-done | bytes 16777232 | tf_op jit(solution)/shard_map/all_gather | solution.py:123
  163.3 46.8 %copy.66 = bf16[64,4,64,512]{2,0,3,1:T(8,128)(2,1)} copy(bf16[64,4,64,512]{3,2,1,0:T(8,128)(2,1)} %all-gather.5.cloned.1.call-done) | data formatting | bytes 33554432 | tf_op jit(solution)/shard_map/all_gather | solution.py:123
  210.1 0.0 copy-done.2
  210.1 24.4 %bitcast_reduce_fusion = (f32[4,4,512]{0,2,1:T(8,128)}, f32[4,512,64,4]{2,3,1,0:T(4,128)}) fusion(pred[64]{0:T(512)(128)(4,1)S(1)} %iota_compare_fusion, bf16[64,4,64,512]{2,0,3,1:T(8,128)(2,1)} %copy.66, bf16[4,4,64,512]{2,0,3,1:T(4,128)(2,1)S(1)} %copy-done.2), kind=kOutput, calls=%fused_computation.1 | convolution fusion | flops 68673536 | bytes 19955776 | tf_op jit(solution)/shard_map/qhdc,khdc->qkhc/dot_general | solution.py:126
  234.5 1.4 broadcast_maximum_fusion
  235.9 30.0 %fusion.20 = f32[4,4,512]{0,2,1:T(8,128)S(1)} fusion(f32[4,4,512]{0,2,1:T(8,128)S(1)} %broadcast_maximum_fusion, f32[4,512,64,4]{2,3,1,0:T(4,128)} %get-tuple-element.9, pred[64]{0:T(512)(128)(4,1)S(1)} %iota_compare_fusion), kind=kLoop, calls=%fused_computation.34 | loop fusion | flops 2613248 | bytes 2162752 | tf_op jit(solution)/shard_map/reduce_sum | solution.py:133
  265.9 0.3 copy.70
  266.2 10.9 %all-gather.3.cloned.1.call-done = bf16[64,4,64,512]{3,2,1,0:T(8,128)(2,1)} async-done(((bf16[4,4,64,512]{3,2,1,0:T(8,128)(2,1)}), bf16[64,4,64,512]{3,2,1,0:T(8,128)(2,1)}) %all-gather.3.cloned.1.call-update) | async-done | bytes 16777232 | tf_op jit(solution)/shard_map/all_gather | solution.py:124
  277.1 46.6 %copy.68 = bf16[64,4,64,512]{2,0,3,1:T(8,128)(2,1)} copy(bf16[64,4,64,512]{3,2,1,0:T(8,128)(2,1)} %all-gather.3.cloned.1.call-done) | data formatting | bytes 33554432 | tf_op jit(solution)/shard_map/all_gather | solution.py:124
  323.7 17.5 %fusion.11 = f32[4,512,64,4]{2,3,1,0:T(4,128)} fusion(bf16[64,4,64,512]{2,0,3,1:T(8,128)(2,1)} %copy.68, f32[4,512,64,4]{2,3,1,0:T(4,128)} %get-tuple-element.9, f32[4,4,512]{0,2,1:T(8,128)S(1)} %broadcast_maximum_fusion, pred[64]{0:T(512)(128)(4,1)S(1)} %iota_compare_fusion), kind=kOutput, calls=%fused_computation.22 | convolution fusion | flops 69730304 | bytes 21004352 | tf_op jit(solution)/shard_map/qkhc,khdc->qhdc/dot_general | solution.py:134
  341.2 3.5 copy.69
  344.7 0.3 fusion.6
  345.0 0.0 copy-done
  345.0 2.3 multiply_reduce_fusion
  347.3 64.6 %psum.7 = f32[]{:T(128)} all-reduce(f32[]{:T(128)} %get-tuple-element.10), channel_id=1, replica_groups=mesh['scene'=8,'frame'=16] {'scene','frame'}, use_global_device_ids=true, to_apply=%region_4.5 | all-reduce | flops 1 | bytes 8 | tf_op jit(solution)/shard_map/psum | solution.py:143
  (4 shorter events, 0.1 us)
Async XLA Ops:
  7.2 337.9 %copy-start = (bf16[256,256]{1,0:T(8,128)(2,1)S(1)}, bf16[256,256]{1,0:T(8,128)(2,1)}, u32[]{:S(2)}) copy-start(bf16[256,256]{1,0:T(8,128)(2,1)} %param.17) | copy-start | bytes 393220
  7.2 156.1 %all-gather.5.cloned.1.call-start = ((), (), s32[]{:S(2)}) async-start(), calls=%async_computation.1 | async-start | bytes 17825792 | tf_op jit(solution)/shard_map/all_gather | solution.py:123
  10.5 2.9 copy-start.3
  16.0 5.0 %copy-start.1 = (bf16[256,128,3,3,3]{0,4,3,2,1:T(4,128)(2,1)S(1)}, bf16[256,128,3,3,3]{0,4,3,2,1:T(4,128)(2,1)}, u32[]{:S(2)}) copy-start(bf16[256,128,3,3,3]{0,4,3,2,1:T(4,128)(2,1)} %reshape.49) | copy-start | bytes 5308420
  30.8 5.8 %copy-start.4 = (bf16[3,256,256]{2,1,0:T(8,128)(2,1)S(1)}, bf16[3,256,256]{2,1,0:T(8,128)(2,1)}, u32[]{:S(2)}) copy-start(bf16[3,256,256]{2,1,0:T(8,128)(2,1)} %param.13) | copy-start | bytes 1179652
  31.2 8.9 %collective-permute-start = (bf16[1,256,512]{2,1,0:T(8,128)(2,1)S(1)}, bf16[1,256,512]{2,1,0:T(8,128)(2,1)S(1)}, u32[]{:S(2)}, u32[]{:S(2)}) collective-permute-start(bf16[1,256,512]{2,1,0:T(8,128)(2,1)S(1)} %get-tuple-element.3), channel_id=1, source_target_pairs={{0,1},{1,2},{2,3},{3,4},{4,5},{5,6},{6,7},{7,8},{8,9},{9,10},{10,1... | collective-permute-start | bytes 786440 | tf_op jit(solution)/shard_map/ppermute | solution.py:25
  35.1 8.7 %collective-permute-start.1 = (bf16[1,256,512]{2,1,0:T(8,128)(2,1)S(1)}, bf16[1,256,512]{2,1,0:T(8,128)(2,1)S(1)}, u32[]{:S(2)}, u32[]{:S(2)}) collective-permute-start(bf16[1,256,512]{2,1,0:T(8,128)(2,1)S(1)} %get-tuple-element.2), channel_id=1, source_target_pairs={{1,0},{2,1},{3,2},{4,3},{5,4},{6,5},{7,6},{8,7},{9,8},{10,9},{11,1... | collective-permute-start | bytes 786440 | tf_op jit(solution)/shard_map/ppermute | solution.py:27
  40.5 4.5 %copy-start.5 = (bf16[256,256]{1,0:T(8,128)(2,1)S(1)}, bf16[256,256]{1,0:T(8,128)(2,1)}, u32[]{:S(2)}) copy-start(bf16[256,256]{1,0:T(8,128)(2,1)} %param.15) | copy-start | bytes 393220
  44.9 1.5 copy-start.6
  46.4 1.6 copy-start.7
  46.4 230.7 %all-gather.3.cloned.1.call-start = ((), (), s32[]{:S(2)}) async-start(), calls=%async_computation | async-start | bytes 17825792 | tf_op jit(solution)/shard_map/all_gather | solution.py:124
  50.9 159.2 %copy-start.2 = (bf16[4,4,64,512]{2,0,3,1:T(4,128)(2,1)S(1)}, bf16[4,4,64,512]{2,0,3,1:T(4,128)(2,1)}, u32[]{:S(2)}) copy-start(bf16[4,4,64,512]{2,0,3,1:T(4,128)(2,1)} %copy.67) | copy-start | bytes 3145732
Sparse Core Ops, SparseCore 0:
  46.6 116.7 all-gather.4
  166.0 111.0 all-gather.2
where the time goes:
time: 423 us; the launch traced here: 421 us
  waiting for transfers between devices  130 us (31%)
  local copies, waits for them, and re-layouts  110 us (26%)
  blocking collectives  64.6 us (15%)
  matrix products  62.2 us (15%)
  other arithmetic  32 us (8%)
  between operations  16.7 us (4%)
  starting transfers between devices  5.51 us (1%)
    all_gather x1, waiting for transfers between devices, shards(): panel_keys = lax.all_gather(key_rows, 'frame', axis=0, tiled=True)  112 us
    psum x1, blocking collectives, shards(): grand_total = lax.psum(squares, ('scene', 'frame'))  64.6 us
    all_gather x1, local copies, waits for them, and re-layouts, shards(): panel_keys = lax.all_gather(key_rows, 'frame', axis=0, tiled=True)  46.8 us
    all_gather x1, local copies, waits for them, and re-layouts, shards(): panel_values = lax.all_gather(value_rows, 'frame', axis=0, tiled=True)  46.6 us
    reduce_sum x1, other arithmetic, shards(): new_sum = jnp.sum(raw_weights, axis=1)  30 us
    dot_general x1, matrix products, shards(): jnp.einsum('qhdc,khdc->qkhc', queries, panel_keys, preferred_element_type...  24.4 us
    dot_general x1, matrix products, shards(): jnp.einsum('qkhc,khdc->qhdc', raw_weights.astype(jnp.bfloat16), panel_val...  17.5 us
    conv_general_dilated x2, matrix products, spatial_conv(): lax.conv_general_dilated(voxels, kernel, (stride, stride, 1), ((1, 1), (1...  12.8 us
  transfers between devices with their start and end apart: 4, of which 4 were waited for; matrix products, arithmetic and copies ran while one was open for 26% of the time, Pallas kernels for 0%

commit v1 on v0

--- a/solution.py
+++ b/solution.py
@@ -12,6 +12,27 @@
 ZD = 8
 CELLS = 512
 NORM_EPS = 1e-06
+
+
+def ring_gather(x, axis, dim):
+    devices, position, rows = (lax.axis_size(axis), lax.axis_index(axis), x.shape[dim])
+    upward = [(i, (i + 1) % devices) for i in range(devices)]
+    backward = [(i, (i - 1) % devices) for i in range(devices)]
+    out = jnp.zeros((*x.shape[:dim], devices * rows, *x.shape[dim + 1 :]), x.dtype)
+    out = lax.dynamic_update_slice_in_dim(out, x, position * rows, axis=dim)
+    from_left = from_right = x
+    half = devices // 2
+    for step in range(1, half + 1):
+        from_left = lax.ppermute(from_left, axis, upward)
+        out = lax.dynamic_update_slice_in_dim(
+            out, from_left, (position - step) % devices * rows, axis=dim
+        )
+        if step < devices - half:
+            from_right = lax.ppermute(from_right, axis, backward)
+            out = lax.dynamic_update_slice_in_dim(
+                out, from_right, (position + step) % devices * rows, axis=dim
+            )
+    return out
 
 
 def extended(cells, sides, width):
@@ -120,7 +141,7 @@
     residual_f = temporal_block(padded, second_maps, temporal_weight)
     queries, key_rows, value_rows = project_rows(residual_f, query_weight, key_weight, value_weight)
     running_max = jnp.full((f_dev, HEADS, CELLS), -1e30, jnp.float32)
-    panel_keys = lax.all_gather(key_rows, "frame", axis=0, tiled=True)
+    panel_keys = ring_gather(key_rows, "frame", 0)
     panel_values = lax.all_gather(value_rows, "frame", axis=0, tiled=True)
     count_keys = panel_keys.shape[0]
     scores = jnp.einsum(

time: 423 us -> 588 us (1.39); the launches traced: 421 us -> 578 us
  local copies, waits for them, and re-layouts: 110 us -> 173 us
  waiting for transfers between devices: 130 us -> 174 us
  starting transfers between devices: 5.51 us -> 42.5 us
  blocking collectives: 64.6 us -> 78.7 us
    ppermute x0 -> x15, waiting for transfers between devices: none -> 167 us  [the longest x8 154 us: ring_gather(): from_left = lax.ppermute(from_left, axis, upward)]
    all_gather x1 -> x0, waiting for transfers between devices: 112 us -> none  [shards(): panel_keys = lax.all_gather(key_rows, 'frame', axis=0, tiled=True)]
    ppermute x0 -> x15, local copies, waits for them, and re-layouts: none -> 50.9 us  [the longest x8 29.4 us: ring_gather(): from_left = lax.ppermute(from_left, axis, upward)]
    all_gather x1 -> x0, local copies, waits for them, and re-layouts: 46.8 us -> none  [shards(): panel_keys = lax.all_gather(key_rows, 'frame', axis=0, tiled=True)]
    dynamic_update_slice x0 -> x16, local copies, waits for them, and re-layouts: none -> 42.7 us  [the longest x8 25.4 us: ring_gather(): lax.dynamic_update_slice_in_dim(out, from_left, (position - step) % devic...]
    ppermute x0 -> x15, starting transfers between devices: none -> 37.1 us  [the longest x7 35.4 us: ring_gather(): from_right = lax.ppermute(from_right, axis, backward)]
    psum x1, blocking collectives: 64.6 us -> 78.7 us  [shards(): grand_total = lax.psum(squares, ('scene', 'frame'))]
    broadcast_in_dim x0 -> x1, local copies, waits for them, and re-layouts: none -> 11.3 us  [ring_gather(): jnp.zeros((*x.shape[:dim], devices * rows, *x.shape[dim + 1:]), x.dtype)]
  transfers between devices with their start and end apart: 4 -> 18, of which waited for: 4 -> 11; matrix products, arithmetic and copies ran while one was open for 26% -> 29% of each run, Pallas kernels for 0% -> 0%
where the time goes in v1:
time: 588 us; the launch traced here: 578 us
  waiting for transfers between devices  174 us (30%)
  local copies, waits for them, and re-layouts  173 us (29%)
  blocking collectives  78.7 us (13%)
  matrix products  61.5 us (10%)
  starting transfers between devices  42.5 us (7%)
  other arithmetic  30.7 us (5%)
  between operations  17.4 us (3%)
    ppermute x8, waiting for transfers between devices, ring_gather(): from_left = lax.ppermute(from_left, axis, upward)  154 us
    psum x1, blocking collectives, shards(): grand_total = lax.psum(squares, ('scene', 'frame'))  78.7 us
    all_gather x1, local copies, waits for them, and re-layouts, shards(): panel_values = lax.all_gather(value_rows, 'frame', axis=0, tiled=True)  46.7 us
    ppermute x7, starting transfers between devices, ring_gather(): from_right = lax.ppermute(from_right, axis, backward)  35.4 us
    reduce_sum x1, other arithmetic, shards(): new_sum = jnp.sum(raw_weights, axis=1)  30 us
    ppermute x8, local copies, waits for them, and re-layouts, ring_gather(): from_left = lax.ppermute(from_left, axis, upward)  29.4 us
    dynamic_update_slice x8, local copies, waits for them, and re-layouts, ring_gather(): lax.dynamic_update_slice_in_dim(out, from_left, (position - step) % devic...  25.4 us
    dot_general x1, matrix products, shards(): jnp.einsum('qhdc,khdc->qkhc', queries, panel_keys, preferred_element_type...  23.6 us
  transfers between devices with their start and end apart: 18, of which 11 were waited for; matrix products, arithmetic and copies ran while one was open for 29% of the time, Pallas kernels for 0%

profile of v1, /device:TPU:1, one launch (start us, length us, event | category | flops | bytes accessed | tf_op | source)
XLA Modules:
  0.0 578.1 jit_solution(18128440267215221369)
XLA Ops:
  7.9 2.6 copy.96
  10.6 2.9 reshape.49
  16.0 5.0 fusion.28
  21.0 7.8 %multiply_convert_fusion = (bf16[4,256,8,8,8]{1,0,4,3,2:T(4,128)(2,1)S(1)}, f32[4,256,8,8,8]{1,0,4,3,2:T(4,128)}) fusion(f32[4]{0:T(128)S(1)} %compare_convert_fusion, bf16[4,128,8,8,8]{1,0,4,3,2:T(4,128)(2,1)S(1)} %fusion.28, bf16[256,128,3,3,3]{0,4,3,2,1:T(4,128)(2,1)S(1)} %copy-done.3), kind=kOutput, calls=%fused_computation.24 | convolution fusion | flops 2794455040 | bytes 5439504 | tf_op jit(solution)/shard_map/conv_general_dilated | solution.py:58
  31.1 4.0 collective-permute-start
  37.0 3.0 collective-permute-done
  40.4 3.4 collective-permute-done.1
  48.1 3.7 collective-permute-start.3
  51.8 25.4 %collective-permute-done.2 = bf16[4,4,64,512]{3,2,1,0:T(8,128)(2,1)S(1)} collective-permute-done((bf16[4,4,64,512]{3,2,1,0:T(8,128)(2,1)S(1)}, bf16[4,4,64,512]{3,2,1,0:T(8,128)(2,1)S(1)}, u32[]{:S(2)}, u32[]{:S(2)}) %collective-permute-start.2) | collective-permute-done | bytes 1048608 | tf_op jit(solution)/shard_map/ppermute | solution.py:26
  77.2 4.1 collective-permute-done.3
  81.3 5.5 collective-permute-start.5
  86.8 25.2 %collective-permute-done.4 = bf16[4,4,64,512]{3,2,1,0:T(8,128)(2,1)S(1)} collective-permute-done((bf16[4,4,64,512]{3,2,1,0:T(8,128)(2,1)S(1)}, bf16[4,4,64,512]{3,2,1,0:T(8,128)(2,1)S(1)}, u32[]{:S(2)}, u32[]{:S(2)}) %collective-permute-start.4) | collective-permute-done | bytes 1048608 | tf_op jit(solution)/shard_map/ppermute | solution.py:26
  112.0 4.8 collective-permute-start.7
  116.8 24.2 %collective-permute-done.6 = bf16[4,4,64,512]{3,2,1,0:T(8,128)(2,1)S(1)} collective-permute-done((bf16[4,4,64,512]{3,2,1,0:T(8,128)(2,1)S(1)}, bf16[4,4,64,512]{3,2,1,0:T(8,128)(2,1)S(1)}, u32[]{:S(2)}, u32[]{:S(2)}) %collective-permute-start.6) | collective-permute-done | bytes 1048608 | tf_op jit(solution)/shard_map/ppermute | solution.py:26
  141.0 3.7 collective-permute-done.7
  144.7 5.5 collective-permute-start.9
  150.2 39.4 %collective-permute-done.8 = bf16[4,4,64,512]{3,2,1,0:T(8,128)(2,1)S(1)} collective-permute-done((bf16[4,4,64,512]{3,2,1,0:T(8,128)(2,1)S(1)}, bf16[4,4,64,512]{3,2,1,0:T(8,128)(2,1)S(1)}, u32[]{:S(2)}, u32[]{:S(2)}) %collective-permute-start.8) | collective-permute-done | bytes 1048608 | tf_op jit(solution)/shard_map/ppermute | solution.py:26
  190.6 2.7 collective-permute-done.9
  193.4 5.5 collective-permute-start.11
  198.9 40.2 %collective-permute-done.10 = bf16[4,4,64,512]{3,2,1,0:T(8,128)(2,1)} collective-permute-done((bf16[4,4,64,512]{3,2,1,0:T(8,128)(2,1)S(1)}, bf16[4,4,64,512]{3,2,1,0:T(8,128)(2,1)}, u32[]{:S(2)}, u32[]{:S(2)}) %collective-permute-start.10) | collective-permute-done | bytes 1048608 | tf_op jit(solution)/shard_map/ppermute | solution.py:26
  239.4 2.6 collective-permute-done.11
  242.0 5.6 collective-permute-start.13
  249.1 2.9 copy.100
  252.0 4.1 copy.116
  256.1 11.3 %broadcast_in_dim.37 = bf16[64,4,64,512]{2,0,3,1:T(8,128)(2,1)} broadcast(bf16[]{:T(256)} %constant.112.clone.1), dimensions={} | broadcast | bytes 16777218 | tf_op jit(solution)/shard_map/broadcast_in_dim | solution.py:21
  267.4 2.1 constant_dynamic-update-slice_fusion.15
  269.5 2.9 copy.101
  272.7 2.1 constant_dynamic-update-slice_fusion.14
  274.8 2.9 copy.102
  277.7 2.2 constant_dynamic-update-slice_fusion.13
  279.9 4.1 copy.103
  283.9 2.9 copy.104
  286.8 3.8 constant_dynamic-update-slice_fusion.12
  290.6 2.2 constant_dynamic-update-slice_fusion.11
  292.8 4.1 copy.105
  296.9 2.9 copy.106
  299.8 3.8 constant_dynamic-update-slice_fusion.10
  303.6 4.7 collective-permute-start.15
  308.3 2.1 constant_dynamic-update-slice_fusion.9
  310.5 4.1 copy.107
  314.5 2.9 copy.108
  317.4 3.7 constant_dynamic-update-slice_fusion.8
  321.2 2.2 constant_dynamic-update-slice_fusion.7
  323.4 4.5 copy.109
  327.8 2.9 copy.110
  330.7 3.8 constant_dynamic-update-slice_fusion.6
  334.5 2.2 constant_dynamic-update-slice_fusion.5
  336.7 4.1 copy.111
  340.8 2.9 copy.112
  343.7 3.7 constant_dynamic-update-slice_fusion.4
  347.4 2.1 constant_dynamic-update-slice_fusion.3
  349.5 2.9 copy.113
  352.5 4.1 copy.114
  356.5 2.2 constant_dynamic-update-slice_fusion.2
  358.7 2.2 constant_dynamic-update-slice_fusion.1
  361.0 2.9 copy.115
  363.9 2.2 constant_dynamic-update-slice_fusion
  366.1 23.6 %bitcast_reduce_fusion = (f32[4,4,512]{0,2,1:T(8,128)S(1)}, f32[4,512,64,4]{2,3,1,0:T(4,128)}) fusion(pred[64]{0:T(512)(128)(4,1)S(1)} %iota_compare_fusion, bf16[64,4,64,512]{2,0,3,1:T(8,128)(2,1)} %constant_dynamic-update-slice_fusion, bf16[4,4,64,512]{2,0,3,1:T(4,128)(2,1)} %copy.116), kind=kOutput, calls=%fused_computation.1 | convolution fusion | flops 68673536 | bytes 19955776 | tf_op jit(solution)/shard_map/qhdc,khdc->qkhc/dot_general | solution.py:147
  389.8 30.0 %fusion.20 = f32[4,4,512]{0,2,1:T(8,128)S(1)} fusion(f32[4,4,512]{0,2,1:T(8,128)S(1)} %broadcast_maximum_fusion, f32[4,512,64,4]{2,3,1,0:T(4,128)} %get-tuple-element.9, pred[64]{0:T(512)(128)(4,1)S(1)} %iota_compare_fusion), kind=kLoop, calls=%fused_computation.34 | loop fusion | flops 2613248 | bytes 2162752 | tf_op jit(solution)/shard_map/reduce_sum | solution.py:154
  420.2 46.7 %copy.117 = bf16[64,4,64,512]{2,0,3,1:T(8,128)(2,1)} copy(bf16[64,4,64,512]{3,2,1,0:T(8,128)(2,1)} %all-gather.2.cloned.1.call-done) | data formatting | bytes 33554432 | tf_op jit(solution)/shard_map/all_gather | solution.py:145
  466.9 17.6 %fusion.11 = f32[4,512,64,4]{2,3,1,0:T(4,128)} fusion(bf16[64,4,64,512]{2,0,3,1:T(8,128)(2,1)} %copy.117, f32[4,512,64,4]{2,3,1,0:T(4,128)} %get-tuple-element.9, f32[4,4,512]{0,2,1:T(8,128)S(1)} %broadcast_maximum_fusion, pred[64]{0:T(512)(128)(4,1)S(1)} %iota_compare_fusion), kind=kOutput, calls=%fused_computation.22 | convolution fusion | flops 69730304 | bytes 21004352 | tf_op jit(solution)/shard_map/qkhc,khdc->qhdc/dot_general | solution.py:155
  484.5 3.5 copy.118
  488.3 2.3 multiply_reduce_fusion
  490.6 78.7 %psum.7 = f32[]{:T(128)} all-reduce(f32[]{:T(128)} %get-tuple-element.10), channel_id=1, replica_groups=mesh['scene'=8,'frame'=16] {'scene','frame'}, use_global_device_ids=true, to_apply=%region_4.5 | all-reduce | flops 1 | bytes 8 | tf_op jit(solution)/shard_map/psum | solution.py:164
  (69 shorter events, 15.2 us)
Async XLA Ops:
  7.2 481.1 %copy-start = (bf16[256,256]{1,0:T(8,128)(2,1)S(1)}, bf16[256,256]{1,0:T(8,128)(2,1)}, u32[]{:S(2)}) copy-start(bf16[256,256]{1,0:T(8,128)(2,1)} %param.17) | copy-start | bytes 393220
  7.2 413.0 %all-gather.2.cloned.1.call-start = ((), (), s32[]{:S(2)}) async-start(), calls=%async_computation | async-start | bytes 17825792 | tf_op jit(solution)/shard_map/all_gather | solution.py:145
  10.5 2.9 copy-start.4
  16.0 5.0 copy-start.3
  30.7 5.8 %copy-start.13 = (bf16[3,256,256]{2,1,0:T(8,128)(2,1)S(1)}, bf16[3,256,256]{2,1,0:T(8,128)(2,1)}, u32[]{:S(2)}) copy-start(bf16[3,256,256]{2,1,0:T(8,128)(2,1)} %param.13) | copy-start | bytes 1179652
  31.1 8.9 %collective-permute-start = (bf16[1,256,512]{2,1,0:T(8,128)(2,1)S(1)}, bf16[1,256,512]{2,1,0:T(8,128)(2,1)S(1)}, u32[]{:S(2)}, u32[]{:S(2)}) collective-permute-start(bf16[1,256,512]{2,1,0:T(8,128)(2,1)S(1)} %get-tuple-element.3), channel_id=1, source_target_pairs={{0,1},{1,2},{2,3},{3,4},{4,5},{5,6},{6,7},{7,8},{8,9},{9,10},{10,1... | collective-permute-start | bytes 786440 | tf_op jit(solution)/shard_map/ppermute | solution.py:46
  35.0 8.8 %collective-permute-start.1 = (bf16[1,256,512]{2,1,0:T(8,128)(2,1)S(1)}, bf16[1,256,512]{2,1,0:T(8,128)(2,1)S(1)}, u32[]{:S(2)}, u32[]{:S(2)}) collective-permute-start(bf16[1,256,512]{2,1,0:T(8,128)(2,1)S(1)} %get-tuple-element.2), channel_id=1, source_target_pairs={{1,0},{2,1},{3,2},{4,3},{5,4},{6,5},{7,6},{8,7},{9,8},{10,9},{11,1... | collective-permute-start | bytes 786440 | tf_op jit(solution)/shard_map/ppermute | solution.py:48
  40.4 4.5 copy-start.14
  44.8 1.5 copy-start.15
  46.3 201.3 %copy-start.16 = (bf16[256,256]{1,0:T(8,128)(2,1)S(1)}, bf16[256,256]{1,0:T(8,128)(2,1)}, u32[]{:S(2)}) copy-start(bf16[256,256]{1,0:T(8,128)(2,1)} %param.14) | copy-start | bytes 393220
  46.8 1.3 copy-start.2
  46.8 30.4 %collective-permute-start.2 = (bf16[4,4,64,512]{3,2,1,0:T(8,128)(2,1)S(1)}, bf16[4,4,64,512]{3,2,1,0:T(8,128)(2,1)S(1)}, u32[]{:S(2)}, u32[]{:S(2)}) collective-permute-start(bf16[4,4,64,512]{3,2,1,0:T(8,128)(2,1)S(1)} %bitcast.87), channel_id=1, source_target_pairs={{0,1},{1,2},{2,3},{3,4},{4,5},{5,6},{6,7},{7,8},{8,9},{9,10},{10,1... | collective-permute-start | bytes 3145736 | tf_op jit(solution)/shard_map/ppermute | solution.py:26
  48.1 33.2 %collective-permute-start.3 = (bf16[4,4,64,512]{3,2,1,0:T(8,128)(2,1)S(1)}, bf16[4,4,64,512]{3,2,1,0:T(8,128)(2,1)S(1)}, u32[]{:S(2)}, u32[]{:S(2)}) collective-permute-start(bf16[4,4,64,512]{3,2,1,0:T(8,128)(2,1)S(1)} %bitcast.88), channel_id=1, source_target_pairs={{0,15},{1,0},{2,1},{3,2},{4,3},{5,4},{6,5},{7,6},{8,7},{9,8},{10,9... | collective-permute-start | bytes 3145736 | tf_op jit(solution)/shard_map/ppermute | solution.py:31
  77.2 9.6 %copy-start.12 = (bf16[4,4,64,512]{3,2,1,0:T(8,128)(2,1)}, bf16[4,4,64,512]{3,2,1,0:T(8,128)(2,1)S(1)}, u32[]{:S(2)}) copy-start(bf16[4,4,64,512]{3,2,1,0:T(8,128)(2,1)S(1)} %collective-permute-done.2) | copy-start | bytes 3145732
  77.2 34.8 %collective-permute-start.4 = (bf16[4,4,64,512]{3,2,1,0:T(8,128)(2,1)S(1)}, bf16[4,4,64,512]{3,2,1,0:T(8,128)(2,1)S(1)}, u32[]{:S(2)}, u32[]{:S(2)}) collective-permute-start(bf16[4,4,64,512]{3,2,1,0:T(8,128)(2,1)S(1)} %collective-permute-done.2), channel_id=1, source_target_pairs={{0,1},{1,2},{2,3},{3,4},{4,5},{5,6},{6,7},{7,8},{8,9},{9,10},{10,1... | collective-permute-start | bytes 3145736 | tf_op jit(solution)/shard_map/ppermute | solution.py:26
  81.3 35.5 %copy-start.6 = (bf16[4,4,64,512]{3,2,1,0:T(8,128)(2,1)}, bf16[4,4,64,512]{3,2,1,0:T(8,128)(2,1)S(1)}, u32[]{:S(2)}) copy-start(bf16[4,4,64,512]{3,2,1,0:T(8,128)(2,1)S(1)} %collective-permute-done.3) | copy-start | bytes 3145732
  81.3 30.7 %collective-permute-start.5 = (bf16[4,4,64,512]{3,2,1,0:T(8,128)(2,1)S(1)}, bf16[4,4,64,512]{3,2,1,0:T(8,128)(2,1)S(1)}, u32[]{:S(2)}, u32[]{:S(2)}) collective-permute-start(bf16[4,4,64,512]{3,2,1,0:T(8,128)(2,1)S(1)} %collective-permute-done.3), channel_id=1, source_target_pairs={{0,15},{1,0},{2,1},{3,2},{4,3},{5,4},{6,5},{7,6},{8,7},{9,8},{10,9... | collective-permute-start | bytes 3145736 | tf_op jit(solution)/shard_map/ppermute | solution.py:31
  112.0 127.0 %copy-start.7 = (bf16[4,4,64,512]{3,2,1,0:T(8,128)(2,1)}, bf16[4,4,64,512]{3,2,1,0:T(8,128)(2,1)S(1)}, u32[]{:S(2)}) copy-start(bf16[4,4,64,512]{3,2,1,0:T(8,128)(2,1)S(1)} %collective-permute-done.4) | copy-start | bytes 3145732
  112.0 28.9 %collective-permute-start.6 = (bf16[4,4,64,512]{3,2,1,0:T(8,128)(2,1)S(1)}, bf16[4,4,64,512]{3,2,1,0:T(8,128)(2,1)S(1)}, u32[]{:S(2)}, u32[]{:S(2)}) collective-permute-start(bf16[4,4,64,512]{3,2,1,0:T(8,128)(2,1)S(1)} %collective-permute-done.4), channel_id=1, source_target_pairs={{0,1},{1,2},{2,3},{3,4},{4,5},{5,6},{6,7},{7,8},{8,9},{9,10},{10,1... | collective-permute-start | bytes 3145736 | tf_op jit(solution)/shard_map/ppermute | solution.py:26
  112.0 127.0 %copy-start.10 = (bf16[4,4,64,512]{3,2,1,0:T(8,128)(2,1)}, bf16[4,4,64,512]{3,2,1,0:T(8,128)(2,1)S(1)}, u32[]{:S(2)}) copy-start(bf16[4,4,64,512]{3,2,1,0:T(8,128)(2,1)S(1)} %collective-permute-done.5) | copy-start | bytes 3145732
  112.0 32.7 %collective-permute-start.7 = (bf16[4,4,64,512]{3,2,1,0:T(8,128)(2,1)S(1)}, bf16[4,4,64,512]{3,2,1,0:T(8,128)(2,1)S(1)}, u32[]{:S(2)}, u32[]{:S(2)}) collective-permute-start(bf16[4,4,64,512]{3,2,1,0:T(8,128)(2,1)S(1)} %collective-permute-done.5), channel_id=1, source_target_pairs={{0,15},{1,0},{2,1},{3,2},{4,3},{5,4},{6,5},{7,6},{8,7},{9,8},{10,9... | collective-permute-start | bytes 3145736 | tf_op jit(solution)/shard_map/ppermute | solution.py:31
  141.0 98.1 %copy-start.8 = (bf16[4,4,64,512]{3,2,1,0:T(8,128)(2,1)}, bf16[4,4,64,512]{3,2,1,0:T(8,128)(2,1)S(1)}, u32[]{:S(2)}) copy-start(bf16[4,4,64,512]{3,2,1,0:T(8,128)(2,1)S(1)} %collective-permute-done.6) | copy-start | bytes 3145732
  141.0 48.6 %collective-permute-start.8 = (bf16[4,4,64,512]{3,2,1,0:T(8,128)(2,1)S(1)}, bf16[4,4,64,512]{3,2,1,0:T(8,128)(2,1)S(1)}, u32[]{:S(2)}, u32[]{:S(2)}) collective-permute-start(bf16[4,4,64,512]{3,2,1,0:T(8,128)(2,1)S(1)} %collective-permute-done.6), channel_id=1, source_target_pairs={{0,1},{1,2},{2,3},{3,4},{4,5},{5,6},{6,7},{7,8},{8,9},{9,10},{10,1... | collective-permute-start | bytes 3145736 | tf_op jit(solution)/shard_map/ppermute | solution.py:26
  144.7 94.3 %copy-start.11 = (bf16[4,4,64,512]{3,2,1,0:T(8,128)(2,1)}, bf16[4,4,64,512]{3,2,1,0:T(8,128)(2,1)S(1)}, u32[]{:S(2)}) copy-start(bf16[4,4,64,512]{3,2,1,0:T(8,128)(2,1)S(1)} %collective-permute-done.7) | copy-start | bytes 3145732
  144.7 48.6 %collective-permute-start.9 = (bf16[4,4,64,512]{3,2,1,0:T(8,128)(2,1)S(1)}, bf16[4,4,64,512]{3,2,1,0:T(8,128)(2,1)S(1)}, u32[]{:S(2)}, u32[]{:S(2)}) collective-permute-start(bf16[4,4,64,512]{3,2,1,0:T(8,128)(2,1)S(1)} %collective-permute-done.7), channel_id=1, source_target_pairs={{0,15},{1,0},{2,1},{3,2},{4,3},{5,4},{6,5},{7,6},{8,7},{9,8},{10,9... | collective-permute-start | bytes 3145736 | tf_op jit(solution)/shard_map/ppermute | solution.py:31
  189.6 1.0 copy-start.5
  190.6 48.4 %collective-permute-start.10 = (bf16[4,4,64,512]{3,2,1,0:T(8,128)(2,1)S(1)}, bf16[4,4,64,512]{3,2,1,0:T(8,128)(2,1)}, u32[]{:S(2)}, u32[]{:S(2)}) collective-permute-start(bf16[4,4,64,512]{3,2,1,0:T(8,128)(2,1)S(1)} %collective-permute-done.8), channel_id=1, source_target_pairs={{0,1},{1,2},{2,3},{3,4},{4,5},{5,6},{6,7},{7,8},{8,9},{9,10},{10,1... | collective-permute-start | bytes 3145736 | tf_op jit(solution)/shard_map/ppermute | solution.py:26
  193.4 54.3 %copy-start.9 = (bf16[4,4,64,512]{3,2,1,0:T(8,128)(2,1)}, bf16[4,4,64,512]{3,2,1,0:T(8,128)(2,1)S(1)}, u32[]{:S(2)}) copy-start(bf16[4,4,64,512]{3,2,1,0:T(8,128)(2,1)S(1)} %collective-permute-done.9) | copy-start | bytes 3145732
  193.4 48.6 %collective-permute-start.11 = (bf16[4,4,64,512]{3,2,1,0:T(8,128)(2,1)S(1)}, bf16[4,4,64,512]{3,2,1,0:T(8,128)(2,1)}, u32[]{:S(2)}, u32[]{:S(2)}) collective-permute-start(bf16[4,4,64,512]{3,2,1,0:T(8,128)(2,1)S(1)} %collective-permute-done.9), channel_id=1, source_target_pairs={{0,15},{1,0},{2,1},{3,2},{4,3},{5,4},{6,5},{7,6},{8,7},{9,8},{10,9... | collective-permute-start | bytes 3145736 | tf_op jit(solution)/shard_map/ppermute | solution.py:31
  239.1 33.3 %collective-permute-start.12 = (bf16[4,4,64,512]{3,2,1,0:T(8,128)(2,1)}, bf16[4,4,64,512]{3,2,1,0:T(8,128)(2,1)}, u32[]{:S(2)}, u32[]{:S(2)}) collective-permute-start(bf16[4,4,64,512]{3,2,1,0:T(8,128)(2,1)} %collective-permute-done.10), channel_id=1, source_target_pairs={{0,1},{1,2},{2,3},{3,4},{4,5},{5,6},{6,7},{7,8},{8,9},{9,10},{10,1... | collective-permute-start | bytes 3145736 | tf_op jit(solution)/shard_map/ppermute | solution.py:26
  242.0 61.6 %collective-permute-start.13 = (bf16[4,4,64,512]{3,2,1,0:T(8,128)(2,1)}, bf16[4,4,64,512]{3,2,1,0:T(8,128)(2,1)}, u32[]{:S(2)}, u32[]{:S(2)}) collective-permute-start(bf16[4,4,64,512]{3,2,1,0:T(8,128)(2,1)} %collective-permute-done.11), channel_id=1, source_target_pairs={{0,15},{1,0},{2,1},{3,2},{4,3},{5,4},{6,5},{7,6},{8,7},{9,8},{10,9... | collective-permute-start | bytes 3145736 | tf_op jit(solution)/shard_map/ppermute | solution.py:31
  272.4 48.8 %collective-permute-start.14 = (bf16[4,4,64,512]{3,2,1,0:T(8,128)(2,1)}, bf16[4,4,64,512]{3,2,1,0:T(8,128)(2,1)}, u32[]{:S(2)}, u32[]{:S(2)}) collective-permute-start(bf16[4,4,64,512]{3,2,1,0:T(8,128)(2,1)} %collective-permute-done.12), channel_id=1, source_target_pairs={{0,1},{1,2},{2,3},{3,4},{4,5},{5,6},{6,7},{7,8},{8,9},{9,10},{10,1... | collective-permute-start | bytes 3145736 | tf_op jit(solution)/shard_map/ppermute | solution.py:26
  303.6 48.8 %collective-permute-start.15 = (bf16[4,4,64,512]{3,2,1,0:T(8,128)(2,1)}, bf16[4,4,64,512]{3,2,1,0:T(8,128)(2,1)}, u32[]{:S(2)}, u32[]{:S(2)}) collective-permute-start(bf16[4,4,64,512]{3,2,1,0:T(8,128)(2,1)} %collective-permute-done.13), channel_id=1, source_target_pairs={{0,15},{1,0},{2,1},{3,2},{4,3},{5,4},{6,5},{7,6},{8,7},{9,8},{10,9... | collective-permute-start | bytes 3145736 | tf_op jit(solution)/shard_map/ppermute | solution.py:31
  321.2 39.8 %collective-permute-start.16 = (bf16[4,4,64,512]{3,2,1,0:T(8,128)(2,1)}, bf16[4,4,64,512]{3,2,1,0:T(8,128)(2,1)}, u32[]{:S(2)}, u32[]{:S(2)}) collective-permute-start(bf16[4,4,64,512]{3,2,1,0:T(8,128)(2,1)} %collective-permute-done.14), channel_id=1, source_target_pairs={{0,1},{1,2},{2,3},{3,4},{4,5},{5,6},{6,7},{7,8},{8,9},{9,10},{10,1... | collective-permute-start | bytes 3145736 | tf_op jit(solution)/shard_map/ppermute | solution.py:26
  356.5 2.2 copy-start.1
Sparse Core Ops, SparseCore 0:
  46.5 209.5 all-gather.1
